TPU v7x, 32 devices: a whole 2x2x4 slice. The times are simulated.
32 devices in a mesh: groups: 2 (over x), slab: 8 (over z, y), ray: 2 (over core).
Axes of the slice: x: 2, y: 2, z: 4, core: 2. Of those that a mesh axis runs over, the one named last changes fastest.
Arguments:
- features: bfloat16 [8, 64, 8, 4096], P('slab', None, None, ('groups', 'ray')), parts along dimension 3, may hold values from -6 to 6
- spacing: float32 [8, 8, 4096], P('slab', None, ('groups', 'ray')), parts along dimension 2, may hold values from 0.004 to 0.04
- live_counts: int32 [8, 4096], P('slab', ('groups', 'ray')), parts along dimension 1, may hold values from 0 to 8
- direction: int32 [4096], P(('groups', 'ray')), parts along dimension 0, may hold values from 0 to 1
- cotangent: float32 [96, 4096], P(None, ('groups', 'ray')), parts along dimension 1, may hold values from -20 to 20
- first_weight: bfloat16 [8, 256, 64], P('slab'), may hold values from -0.75 to 0.75
- first_bias: float32 [8, 256], P('slab'), may hold values from -3 to 3
- second_weight: bfloat16 [8, 256, 256], P('slab'), may hold values from -0.375 to 0.375
- second_bias: float32 [8, 256], P('slab'), may hold values from -3 to 3
- color_weight: bfloat16 [8, 96, 256], P('slab'), may hold values from -0.375 to 0.375
- color_bias: float32 [8, 96], P('slab'), may hold values from -4 to 4
- sigma_weight: bfloat16 [8, 256], P('slab'), may hold values from -0.375 to 0.375
- sigma_bias: float32 [8], P('slab'), may hold values from -1 to 1
Outputs:
- feature_grad: bfloat16 [8, 64, 8, 4096], P('slab', None, None, ('groups', 'ray')), parts along dimension 3
- density_grad: float32 [8, 8, 4096], P('slab', None, ('groups', 'ray')), parts along dimension 2
- radiance_grad: bfloat16 [8, 96, 8, 4096], P('slab', None, None, ('groups', 'ray')), parts along dimension 3
- first_grad: float32 [16, 256, 64], P(('groups', 'slab'), 'ray'), parts along dimension 0
- second_grad: float32 [16, 256, 256], P(('groups', 'slab'), 'ray'), parts along dimension 0
- color_grad: float32 [16, 256, 96], P(('groups', 'slab'), 'ray'), parts along dimension 0
- sigma_grad: float32 [16, 256], P(('groups', 'slab'), 'ray'), parts along dimension 0
There are 2 independent parts, one for each index of `groups`. A program takes and returns all parts, laid end to end along the dimension named above; an argument that names none is the same for every part. Nothing has to cross between parts.
Inputs may be any that keep to these rules, and one draw needn't show every extreme that they name: The first live_counts slots of a ray in a slab hold its samples. `direction`: 0: the ray meets the slabs in rising index order; 1: in falling order.
All inputs are finite; a program needn't handle non-finite values.
Results may differ from a plain program's by a relative error of at most 0.0067.
Values sent between devices are 32-bit elements; how exact they have to be, the bound alone decides.
A program may use at most 128 MiB of HBM per device.

v0:
```python
import jax
import jax.numpy as jnp
from jax import lax
from jax.sharding import PartitionSpec as P


def silu_slope(values):
    gate = jax.nn.sigmoid(values)
    return gate * (1.0 + values * (1.0 - gate))


def hidden_layers(inputs, weight_a, bias_a, weight_b, bias_b):
    first_pre = jnp.dot(weight_a, inputs, preferred_element_type=jnp.float32) + bias_a[:, None]
    first_act = jax.nn.silu(first_pre).astype(jnp.bfloat16)
    second_pre = jnp.dot(weight_b, first_act, preferred_element_type=jnp.float32) + bias_b[:, None]
    second_act = jax.nn.silu(second_pre).astype(jnp.bfloat16)
    return (first_pre, first_act, second_pre, second_act)


def body(
    features,
    spacing,
    live_counts,
    direction,
    cotangent,
    first_weight,
    first_bias,
    second_weight,
    second_bias,
    color_weight,
    color_bias,
    sigma_weight,
    sigma_bias,
):
    inputs = features[0]
    slots = inputs.shape[1]
    weight_a = first_weight[0]
    bias_a = first_bias[0]
    weight_b = second_weight[0]
    bias_b = second_bias[0]
    weight_c = color_weight[0]
    bias_c = color_bias[0]
    weight_d = sigma_weight[0]
    bias_d = sigma_bias[0]
    color_list = []
    density_list = []
    stored_layers = []
    for position in range(slots):
        layer_values = hidden_layers(inputs[:, position, :], weight_a, bias_a, weight_b, bias_b)
        stored_layers.append(layer_values)
        second_act = layer_values[3]
        logits = jnp.dot(weight_c, second_act, preferred_element_type=jnp.float32) + bias_c[:, None]
        color_list.append(jax.nn.sigmoid(logits))
        density_list.append(
            jnp.dot(weight_d, second_act, preferred_element_type=jnp.float32) + bias_d
        )
    radiance = jnp.stack(color_list, axis=1)
    raw_density = jnp.stack(density_list, axis=0)
    gaps = spacing[0]
    live = (lax.broadcasted_iota(jnp.int32, raw_density.shape, 0) < live_counts[0][None, :]).astype(
        jnp.float32
    )
    depth = jax.nn.softplus(raw_density) * gaps * live
    inside = jnp.cumsum(depth, axis=0) - depth
    slab_depth = jnp.sum(depth, axis=0)
    opacity = 1.0 - jnp.exp(-depth)
    local = jnp.sum((jnp.exp(-inside) * opacity)[None] * radiance, axis=1)
    ascend = direction == 0
    descend = jnp.logical_not(ascend)
    local_proj = jnp.sum(cotangent * local, axis=0)
    depths, lights = (
        lax.all_gather(slab_depth[None], "slab", axis=0, tiled=True),
        lax.all_gather(local_proj[None], "slab", axis=0, tiled=True),
    )
    slab_index = lax.axis_index("slab")
    before_all = jnp.cumsum(depths, axis=0) - depths
    own_before = lax.dynamic_index_in_dim(before_all, slab_index, 0, keepdims=False)
    total_depth = jnp.sum(depths, axis=0)
    prefix = jnp.where(ascend, own_before, total_depth - own_before - slab_depth)
    slab_order = lax.broadcasted_iota(jnp.int32, depths.shape, 0)
    upward = jnp.logical_and(slab_order > slab_index, ascend[None])
    downward = jnp.logical_and(slab_order < slab_index, descend[None])
    between = jnp.where(
        upward,
        before_all - own_before[None] - slab_depth[None],
        own_before[None] - before_all - depths,
    )
    chosen = jnp.logical_or(upward, downward)
    factor = jnp.where(chosen, jnp.exp(-jnp.maximum(between, 0.0)), 0.0)
    behind_sum = jnp.sum(factor * lights, axis=0)
    behind_out = jnp.exp(-(prefix + slab_depth)) * behind_sum
    transmit = jnp.exp(-(prefix[None] + inside))
    sample_weight = transmit * opacity
    radiance_full = sample_weight[None] * cotangent[:, None, :]
    radiance_grad = radiance_full.astype(jnp.bfloat16)
    projected = jnp.sum(cotangent[:, None, :] * radiance, axis=0)
    carried = sample_weight * projected
    behind_in = jnp.sum(carried, axis=0, keepdims=True) - jnp.cumsum(carried, axis=0)
    density_grad = (
        (transmit * jnp.exp(-depth) * projected - behind_in - behind_out[None]) * gaps * live
    )
    logit_grad = (radiance_full * radiance * (1.0 - radiance)).astype(jnp.bfloat16)
    raw_grad = (density_grad * jax.nn.sigmoid(raw_density)).astype(jnp.bfloat16)
    hidden = weight_a.shape[0]
    first_sum = jnp.zeros((hidden, inputs.shape[0]), jnp.float32)
    second_sum = jnp.zeros((hidden, hidden), jnp.float32)
    color_sum = jnp.zeros((hidden, weight_c.shape[0]), jnp.float32)
    sigma_sum = jnp.zeros((hidden,), jnp.float32)
    feature_list = []
    column_d = weight_d[:, None].astype(jnp.float32)
    for position in range(slots):
        block_inputs = inputs[:, position, :]
        first_pre, first_act, second_pre, second_act = stored_layers[position]
        logit_block = logit_grad[:, position, :]
        raw_block = raw_grad[position]
        hidden_two = jnp.einsum(
            "ch,cr->hr", weight_c, logit_block, preferred_element_type=jnp.float32
        )
        hidden_two = hidden_two + column_d * raw_block[None, :].astype(jnp.float32)
        second_delta = (hidden_two * silu_slope(second_pre)).astype(jnp.bfloat16)
        hidden_one = jnp.einsum(
            "gh,gr->hr", weight_b, second_delta, preferred_element_type=jnp.float32
        )
        first_delta = (hidden_one * silu_slope(first_pre)).astype(jnp.bfloat16)
        feature_list.append(
            jnp.einsum(
                "hf,hr->fr", weight_a, first_delta, preferred_element_type=jnp.float32
            ).astype(jnp.bfloat16)
        )
        first_sum = first_sum + jnp.einsum(
            "hr,fr->hf", first_delta, block_inputs, preferred_element_type=jnp.float32
        )
        second_sum = second_sum + jnp.einsum(
            "hr,gr->hg", second_delta, first_act, preferred_element_type=jnp.float32
        )
        color_sum = color_sum + jnp.einsum(
            "hr,cr->hc", second_act, logit_block, preferred_element_type=jnp.float32
        )
        sigma_sum = sigma_sum + jnp.einsum(
            "hr,r->h", second_act, raw_block, preferred_element_type=jnp.float32
        )
    feature_grad = jnp.stack(feature_list, axis=1)
    totals = (
        lax.psum_scatter(first_sum, "ray", scatter_dimension=0, tiled=True),
        lax.psum_scatter(second_sum, "ray", scatter_dimension=0, tiled=True),
        lax.psum_scatter(color_sum, "ray", scatter_dimension=0, tiled=True),
        lax.psum_scatter(sigma_sum, "ray", scatter_dimension=0, tiled=True),
    )
    return (
        feature_grad[None],
        density_grad[None],
        radiance_grad[None],
        totals[0][None],
        totals[1][None],
        totals[2][None],
        totals[3][None],
    )


def solution(mesh):
    in_specs = (
        P("slab", None, None, ("groups", "ray")),
        P("slab", None, ("groups", "ray")),
        P("slab", ("groups", "ray")),
        P(("groups", "ray")),
        P(None, ("groups", "ray")),
        P("slab", None, None),
        P("slab", None),
        P("slab", None, None),
        P("slab", None),
        P("slab", None, None),
        P("slab", None),
        P("slab", None),
        P("slab"),
    )
    out_specs = (
        P("slab", None, None, ("groups", "ray")),
        P("slab", None, ("groups", "ray")),
        P("slab", None, None, ("groups", "ray")),
        P(("groups", "slab"), "ray", None),
        P(("groups", "slab"), "ray", None),
        P(("groups", "slab"), "ray", None),
        P(("groups", "slab"), "ray"),
    )
    return jax.shard_map(body, mesh=mesh, in_specs=in_specs, out_specs=out_specs, check_vma=False)
```

profile of v0, /device:TPU:0, one launch (start us, length us, event | category | flops | bytes accessed | tf_op | source)
XLA Modules:
  0.0 173.8 jit_solution(8739929428887186807)
XLA Ops:
  7.3 1.8 %copy.122 = bf16[1,64,8,1024]{3,1,2,0:T(8,128)(2,1)S(1)} copy(bf16[1,64,8,1024]{3,2,1,0:T(8,128)(2,1)} %param.13) | data formatting | bytes 2097152 | tf_op args[0]
  9.1 2.2 %multiply_convert_fusion.17 = (bf16[256,1024]{1,0:T(8,128)(2,1)S(1)}, f32[256,1024]{1,0:T(8,128)}) fusion(f32[256]{0:T(256)} %bitcast.623, bf16[64,8,1024]{2,0,1:T(8,128)(2,1)S(1)} %bitcast.602, bf16[1,256,64]{1,2,0:T(8,128)(2,1)} %param.18), kind=kOutput, calls=%fused_computation.216 | convolution fusion | flops 35127296 | bytes 1737728 | tf_op jit(solution)/shard_map/dot_general | solution.py:13
  13.6 1.4 multiply_convert_fusion.16
  15.0 1.5 multiply_convert_fusion.14
  17.5 1.6 multiply_convert_fusion.10
  19.3 1.5 multiply_convert_fusion.12
  21.0 1.5 multiply_convert_fusion.6
  22.7 1.5 multiply_convert_fusion.8
  24.4 1.5 multiply_convert_fusion.2
  26.1 1.5 multiply_convert_fusion.4
  30.5 1.6 multiply_reduce_fusion
  32.2 32.2 %all-gather.1 = f32[8192]{0:T(1024)S(1)} all-gather(f32[1024]{0:T(1024)S(1)} %multiply_reduce_fusion.2), channel_id=3, replica_groups=mesh['groups'=2,'slab'=8,'ray'=2] {'slab'}, dimensions={0}, use_global_device_ids=true | all-gather | bytes 36864 | tf_op jit(solution)/shard_map/all_gather | solution.py:73
  64.4 0.6 reshape.592
  65.0 32.2 %all-gather = f32[8192]{0:T(1024)} all-gather(f32[1024]{0:T(1024)S(1)} %get-tuple-element.46), channel_id=2, replica_groups=mesh['groups'=2,'slab'=8,'ray'=2] {'slab'}, dimensions={0}, use_global_device_ids=true | all-gather | bytes 36864 | tf_op jit(solution)/shard_map/all_gather | solution.py:72
  97.2 0.8 reshape.591
  97.9 0.6 reduce_window_sum.22
  98.6 1.4 sub.141
  100.5 1.3 fusion.220
  101.7 0.8 constant_dynamic-slice_fusion
  102.5 0.9 fusion.151
  103.4 1.3 exponential_multiply_fusion
  104.7 1.2 fusion.219
  105.9 0.8 reduce_window_sum.30
  106.7 0.8 fusion.162
  107.5 1.4 fusion.159
  109.0 0.7 reduce
  109.7 1.6 multiply_convert_fusion.1
  111.4 0.6 fusion.38
  112.0 1.2 copy-done.61
  114.0 0.6 copy-done.83
  115.1 0.7 copy-done.58
  116.6 0.6 copy-done.80
  117.2 0.6 fusion.36
  117.8 0.7 copy-done.55
  119.2 0.6 copy-done.81
  120.4 0.7 copy-done.52
  121.9 0.6 copy-done.78
  122.5 0.6 fusion.34
  123.1 0.7 copy-done.49
  124.5 0.6 copy-done.79
  125.7 0.7 copy-done.46
  127.2 0.6 copy-done.77
  128.3 0.7 copy-done.43
  129.8 0.6 copy-done.75
  131.0 0.6 copy-done.76
  134.6 0.9 convolution_add_fusion.38
  135.6 1.5 fusion.112
  139.0 0.9 convolution_add_fusion.31
  140.3 1.6 fusion.223
  141.9 1.9 %convolution_add_fusion.30 = f32[256,256]{1,0:T(8,128)S(1)} fusion(f32[256,256]{1,0:T(8,128)S(1)} %fusion.223, bf16[256,1024]{1,0:T(8,128)(2,1)} %copy-done.84, f32[256,1024]{1,0:T(8,128)} %copy-done.60), kind=kOutput, calls=%fused_computation.146 | convolution fusion | flops 135593984 | bytes 2097152 | tf_op jit(solution)/shard_map/hr,gr->hg/dot_general | solution.py:133
  144.3 0.7 copy-done.56
  145.7 0.7 copy-done.53
  147.0 0.7 copy-done.50
  148.4 0.7 copy-done.47
  149.8 0.7 copy-done.44
  150.6 1.2 convolution_add_fusion.24
  151.9 1.4 fusion.97
  153.5 1.4 fusion.181
  158.1 1.5 copy.96
  159.6 0.6 dynamic-slice
  160.9 2.5 %all-reduce = f32[256]{0:T(256)S(1)} all-reduce(f32[256]{0:T(256)S(1)} %add_add_fusion), channel_id=7, replica_groups=mesh['groups'=2,'slab'=8,'ray'=2] {'ray'}, use_global_device_ids=true, to_apply=%region_13.14.clone | all-reduce | flops 256 | bytes 2048
  163.3 0.6 dynamic-slice_bitcast_fusion
  163.9 1.4 multiply_convert_fusion
  165.4 1.9 %reduce-scatter.6.cloned.1.call-done = f32[128,256]{1,0:T(8,128)} async-done(((f32[256,256]{1,0:T(8,128)}), f32[128,256]{1,0:T(8,128)}) %reduce-scatter.6.cloned.1.call-update) | async-done | bytes 131088 | tf_op jit(solution)/shard_map/reduce_scatter | solution.py:145
  (272 shorter events, 26.7 us)
Async XLA Ops:
  7.2 6.4 %copy-start = (bf16[1,256,256]{2,1,0:T(8,128)(2,1)S(1)}, bf16[1,256,256]{2,1,0:T(8,128)(2,1)}, u32[]{:S(2)}) copy-start(bf16[1,256,256]{2,1,0:T(8,128)(2,1)} %param.20) | copy-start | bytes 393220
  7.2 4.0 %copy-start.68 = (f32[1,256]{1,0:T(1,128)S(1)}, f32[1,256]{1,0:T(1,128)}, u32[]{:S(2)}) copy-start(f32[1,256]{1,0:T(1,128)} %param.19) | copy-start | bytes 3076
  7.2 4.0 %copy-start.3 = (bf16[1,256,64]{1,2,0:T(8,128)(2,1)S(1)}, bf16[1,256,64]{1,2,0:T(8,128)(2,1)}, u32[]{:S(2)}) copy-start(bf16[1,256,64]{1,2,0:T(8,128)(2,1)} %param.18) | copy-start | bytes 98308
  7.2 158.2 %reduce-scatter.4.cloned.1.call-start = ((), (), s32[]{:S(2)}) async-start(), calls=%async_computation.3 | async-start | bytes 98304 | tf_op jit(solution)/shard_map/reduce_scatter | solution.py:144
  9.1 4.2 %copy-start.1 = (bf16[1,64,8,1024]{3,1,2,0:T(8,128)(2,1)}, bf16[1,64,8,1024]{3,1,2,0:T(8,128)(2,1)S(1)}, u32[]{:S(2)}) copy-start(bf16[1,64,8,1024]{3,1,2,0:T(8,128)(2,1)S(1)} %copy.122) | copy-start | bytes 3145732
  11.2 2.4 %copy-start.63 = (bf16[256,1024]{1,0:T(8,128)(2,1)}, bf16[256,1024]{1,0:T(8,128)(2,1)S(1)}, u32[]{:S(2)}) copy-start(bf16[256,1024]{1,0:T(8,128)(2,1)S(1)} %get-tuple-element.50) | copy-start | bytes 1572868
  11.5 3.4 %copy-start.60 = (f32[256,1024]{1,0:T(8,128)}, f32[256,1024]{1,0:T(8,128)S(1)}, u32[]{:S(2)}) copy-start(f32[256,1024]{1,0:T(8,128)S(1)} %convolution_add_fusion.14) | copy-start | bytes 3145732
  11.9 5.7 %copy-start.54 = (f32[256,1024]{1,0:T(8,128)}, f32[256,1024]{1,0:T(8,128)S(1)}, u32[]{:S(2)}) copy-start(f32[256,1024]{1,0:T(8,128)S(1)} %convolution_add_fusion.12) | copy-start | bytes 3145732
  11.9 1.7 copy-start.72
  12.2 7.1 %copy-start.57 = (f32[256,1024]{1,0:T(8,128)}, f32[256,1024]{1,0:T(8,128)S(1)}, u32[]{:S(2)}) copy-start(f32[256,1024]{1,0:T(8,128)S(1)} %convolution_add_fusion.13) | copy-start | bytes 3145732
  12.6 8.4 %copy-start.48 = (f32[256,1024]{1,0:T(8,128)}, f32[256,1024]{1,0:T(8,128)S(1)}, u32[]{:S(2)}) copy-start(f32[256,1024]{1,0:T(8,128)S(1)} %convolution_add_fusion.10) | copy-start | bytes 3145732
  12.9 9.8 %copy-start.51 = (f32[256,1024]{1,0:T(8,128)}, f32[256,1024]{1,0:T(8,128)S(1)}, u32[]{:S(2)}) copy-start(f32[256,1024]{1,0:T(8,128)S(1)} %convolution_add_fusion.11) | copy-start | bytes 3145732
  13.2 11.1 %copy-start.42 = (f32[256,1024]{1,0:T(8,128)}, f32[256,1024]{1,0:T(8,128)S(1)}, u32[]{:S(2)}) copy-start(f32[256,1024]{1,0:T(8,128)S(1)} %convolution_add_fusion.8) | copy-start | bytes 3145732
  13.6 12.5 %copy-start.45 = (f32[256,1024]{1,0:T(8,128)}, f32[256,1024]{1,0:T(8,128)S(1)}, u32[]{:S(2)}) copy-start(f32[256,1024]{1,0:T(8,128)S(1)} %convolution_add_fusion.9) | copy-start | bytes 3145732
  15.0 12.8 %copy-start.25 = (bf16[256,1024]{1,0:T(8,128)(2,1)}, bf16[256,1024]{1,0:T(8,128)(2,1)S(1)}, u32[]{:S(2)}) copy-start(bf16[256,1024]{1,0:T(8,128)(2,1)S(1)} %get-tuple-element.52) | copy-start | bytes 1572868
  15.0 2.2 %copy-start.65 = (bf16[1,256]{1,0:T(2,128)(2,1)S(1)}, bf16[1,256]{1,0:T(2,128)(2,1)}, u32[]{:S(2)}) copy-start(bf16[1,256]{1,0:T(2,128)(2,1)} %param.24) | copy-start | bytes 1540
  16.5 11.6 %copy-start.8 = (bf16[256,1024]{1,0:T(8,128)(2,1)}, bf16[256,1024]{1,0:T(8,128)(2,1)S(1)}, u32[]{:S(2)}) copy-start(bf16[256,1024]{1,0:T(8,128)(2,1)S(1)} %get-tuple-element.54) | copy-start | bytes 1572868
  19.1 9.5 %copy-start.10 = (bf16[256,1024]{1,0:T(8,128)(2,1)}, bf16[256,1024]{1,0:T(8,128)(2,1)S(1)}, u32[]{:S(2)}) copy-start(bf16[256,1024]{1,0:T(8,128)(2,1)S(1)} %get-tuple-element.58) | copy-start | bytes 1572868
  20.8 7.6 %copy-start.12 = (bf16[256,1024]{1,0:T(8,128)(2,1)}, bf16[256,1024]{1,0:T(8,128)(2,1)S(1)}, u32[]{:S(2)}) copy-start(bf16[256,1024]{1,0:T(8,128)(2,1)S(1)} %get-tuple-element.56) | copy-start | bytes 1572868
  22.5 6.7 %copy-start.14 = (bf16[256,1024]{1,0:T(8,128)(2,1)}, bf16[256,1024]{1,0:T(8,128)(2,1)S(1)}, u32[]{:S(2)}) copy-start(bf16[256,1024]{1,0:T(8,128)(2,1)S(1)} %get-tuple-element.62) | copy-start | bytes 1572868
  24.2 4.8 %copy-start.17 = (bf16[256,1024]{1,0:T(8,128)(2,1)}, bf16[256,1024]{1,0:T(8,128)(2,1)S(1)}, u32[]{:S(2)}) copy-start(bf16[256,1024]{1,0:T(8,128)(2,1)S(1)} %get-tuple-element.60) | copy-start | bytes 1572868
  25.9 4.0 %copy-start.20 = (bf16[256,1024]{1,0:T(8,128)(2,1)}, bf16[256,1024]{1,0:T(8,128)(2,1)S(1)}, u32[]{:S(2)}) copy-start(bf16[256,1024]{1,0:T(8,128)(2,1)S(1)} %get-tuple-element.66) | copy-start | bytes 1572868
  26.1 1.7 copy-start.70
  26.1 1.7 copy-start.73
  27.6 2.0 %copy-start.23 = (bf16[256,1024]{1,0:T(8,128)(2,1)}, bf16[256,1024]{1,0:T(8,128)(2,1)S(1)}, u32[]{:S(2)}) copy-start(bf16[256,1024]{1,0:T(8,128)(2,1)S(1)} %get-tuple-element.64) | copy-start | bytes 1572868
  101.7 1.7 copy-start.69
  104.7 2.0 %copy-start.66 = (f32[1024]{0:T(1024)}, f32[1024]{0:T(1024)S(1)}, u32[]{:S(2)}) copy-start(f32[1024]{0:T(1024)S(1)} %get-tuple-element.43) | copy-start | bytes 12292
  108.9 2.4 %copy-start.71 = (bf16[1,96,256]{2,1,0:T(8,128)(2,1)S(1)}, bf16[1,96,256]{2,1,0:T(8,128)(2,1)}, u32[]{:S(2)}) copy-start(bf16[1,96,256]{2,1,0:T(8,128)(2,1)} %param.22) | copy-start | bytes 147460
  111.3 18.5 %copy-start.4 = (bf16[96,8,1024]{2,0,1:T(8,128)(2,1)}, bf16[96,8,1024]{2,0,1:T(8,128)(2,1)S(1)}, u32[]{:S(2)}) copy-start(bf16[96,8,1024]{2,0,1:T(8,128)(2,1)S(1)} %multiply_convert_fusion.1) | copy-start | bytes 4718596
  111.4 1.8 %copy-start.61 = (f32[256,1024]{1,0:T(8,128)S(1)}, f32[256,1024]{1,0:T(8,128)}, u32[]{:S(2)}) copy-start(f32[256,1024]{1,0:T(8,128)} %copy-done.60) | copy-start | bytes 3145732
  113.7 19.1 %copy-start.27 = (bf16[256,1024]{1,0:T(8,128)(2,1)}, bf16[256,1024]{1,0:T(8,128)(2,1)S(1)}, u32[]{:S(2)}) copy-start(bf16[256,1024]{1,0:T(8,128)(2,1)S(1)} %fusion.41) | copy-start | bytes 1572868
  116.3 16.8 %copy-start.29 = (bf16[256,1024]{1,0:T(8,128)(2,1)}, bf16[256,1024]{1,0:T(8,128)(2,1)S(1)}, u32[]{:S(2)}) copy-start(bf16[256,1024]{1,0:T(8,128)(2,1)S(1)} %fusion.42) | copy-start | bytes 1572868
  119.0 14.4 %copy-start.31 = (bf16[256,1024]{1,0:T(8,128)(2,1)}, bf16[256,1024]{1,0:T(8,128)(2,1)S(1)}, u32[]{:S(2)}) copy-start(bf16[256,1024]{1,0:T(8,128)(2,1)S(1)} %fusion.43) | copy-start | bytes 1572868
  121.6 12.1 %copy-start.33 = (bf16[256,1024]{1,0:T(8,128)(2,1)}, bf16[256,1024]{1,0:T(8,128)(2,1)S(1)}, u32[]{:S(2)}) copy-start(bf16[256,1024]{1,0:T(8,128)(2,1)S(1)} %fusion.44) | copy-start | bytes 1572868
  124.2 9.7 %copy-start.35 = (bf16[256,1024]{1,0:T(8,128)(2,1)}, bf16[256,1024]{1,0:T(8,128)(2,1)S(1)}, u32[]{:S(2)}) copy-start(bf16[256,1024]{1,0:T(8,128)(2,1)S(1)} %fusion.45) | copy-start | bytes 1572868
  126.9 7.4 %copy-start.37 = (bf16[256,1024]{1,0:T(8,128)(2,1)}, bf16[256,1024]{1,0:T(8,128)(2,1)S(1)}, u32[]{:S(2)}) copy-start(bf16[256,1024]{1,0:T(8,128)(2,1)S(1)} %fusion.46) | copy-start | bytes 1572868
  129.8 4.8 %copy-start.39 = (bf16[256,1024]{1,0:T(8,128)(2,1)}, bf16[256,1024]{1,0:T(8,128)(2,1)S(1)}, u32[]{:S(2)}) copy-start(bf16[256,1024]{1,0:T(8,128)(2,1)S(1)} %fusion.47) | copy-start | bytes 1572868
  131.0 1.8 %copy-start.64 = (bf16[256,1024]{1,0:T(8,128)(2,1)}, bf16[256,1024]{1,0:T(8,128)(2,1)S(1)}, u32[]{:S(2)}) copy-start(bf16[256,1024]{1,0:T(8,128)(2,1)S(1)} %fusion.39) | copy-start | bytes 1572868
  132.5 2.1 %copy-start.41 = (bf16[256,1024]{1,0:T(8,128)(2,1)}, bf16[256,1024]{1,0:T(8,128)(2,1)S(1)}, u32[]{:S(2)}) copy-start(bf16[256,1024]{1,0:T(8,128)(2,1)S(1)} %fusion.40) | copy-start | bytes 1572868
  132.5 3.1 %copy-start.5 = (bf16[96,8,1024]{2,0,1:T(8,128)(2,1)S(1)}, bf16[96,8,1024]{2,0,1:T(8,128)(2,1)}, u32[]{:S(2)}) copy-start(bf16[96,8,1024]{2,0,1:T(8,128)(2,1)} %copy-done.4) | copy-start | bytes 4718596
  132.8 4.3 %copy-start.9 = (bf16[256,1024]{1,0:T(8,128)(2,1)S(1)}, bf16[256,1024]{1,0:T(8,128)(2,1)}, u32[]{:S(2)}) copy-start(bf16[256,1024]{1,0:T(8,128)(2,1)} %copy-done.8) | copy-start | bytes 1572868
  133.1 4.4 %copy-start.13 = (bf16[256,1024]{1,0:T(8,128)(2,1)S(1)}, bf16[256,1024]{1,0:T(8,128)(2,1)}, u32[]{:S(2)}) copy-start(bf16[256,1024]{1,0:T(8,128)(2,1)} %copy-done.12) | copy-start | bytes 1572868
  133.4 4.4 %copy-start.11 = (bf16[256,1024]{1,0:T(8,128)(2,1)S(1)}, bf16[256,1024]{1,0:T(8,128)(2,1)}, u32[]{:S(2)}) copy-start(bf16[256,1024]{1,0:T(8,128)(2,1)} %copy-done.10) | copy-start | bytes 1572868
  135.5 29.8 %reduce-scatter.8.cloned.1.call-start = ((), (), s32[]{:S(2)}) async-start(), calls=%async_computation.5 | async-start | bytes 147456 | tf_op jit(solution)/shard_map/reduce_scatter | solution.py:146
  135.6 2.5 %copy-start.18 = (bf16[256,1024]{1,0:T(8,128)(2,1)S(1)}, bf16[256,1024]{1,0:T(8,128)(2,1)}, u32[]{:S(2)}) copy-start(bf16[256,1024]{1,0:T(8,128)(2,1)} %copy-done.17) | copy-start | bytes 1572868
  135.6 2.8 %copy-start.15 = (bf16[256,1024]{1,0:T(8,128)(2,1)S(1)}, bf16[256,1024]{1,0:T(8,128)(2,1)}, u32[]{:S(2)}) copy-start(bf16[256,1024]{1,0:T(8,128)(2,1)} %copy-done.14) | copy-start | bytes 1572868
  135.6 3.1 %copy-start.24 = (bf16[256,1024]{1,0:T(8,128)(2,1)S(1)}, bf16[256,1024]{1,0:T(8,128)(2,1)}, u32[]{:S(2)}) copy-start(bf16[256,1024]{1,0:T(8,128)(2,1)} %copy-done.23) | copy-start | bytes 1572868
  135.6 3.4 %copy-start.21 = (bf16[256,1024]{1,0:T(8,128)(2,1)S(1)}, bf16[256,1024]{1,0:T(8,128)(2,1)}, u32[]{:S(2)}) copy-start(bf16[256,1024]{1,0:T(8,128)(2,1)} %copy-done.20) | copy-start | bytes 1572868
  140.0 3.8 %copy-start.59 = (f32[256,1024]{1,0:T(8,128)S(1)}, f32[256,1024]{1,0:T(8,128)}, u32[]{:S(2)}) copy-start(f32[256,1024]{1,0:T(8,128)} %copy-done.57) | copy-start | bytes 3145732
  140.0 27.3 %reduce-scatter.6.cloned.1.call-start = ((), (), s32[]{:S(2)}) async-start(), calls=%async_computation.4 | async-start | bytes 393216 | tf_op jit(solution)/shard_map/reduce_scatter | solution.py:145
  140.3 3.5 %copy-start.86 = (bf16[256,1024]{1,0:T(8,128)(2,1)S(1)}, bf16[256,1024]{1,0:T(8,128)(2,1)}, u32[]{:S(2)}) copy-start(bf16[256,1024]{1,0:T(8,128)(2,1)} %copy-done.85) | copy-start | bytes 1572868
  150.6 2.7 %copy-start.22 = (bf16[256,1024]{1,0:T(8,128)(2,1)S(1)}, bf16[256,1024]{1,0:T(8,128)(2,1)}, u32[]{:S(2)}) copy-start(bf16[256,1024]{1,0:T(8,128)(2,1)} %copy-done.20) | copy-start | bytes 1572868
  150.6 4.3 %copy-start.16 = (bf16[256,1024]{1,0:T(8,128)(2,1)S(1)}, bf16[256,1024]{1,0:T(8,128)(2,1)}, u32[]{:S(2)}) copy-start(bf16[256,1024]{1,0:T(8,128)(2,1)} %copy-done.14) | copy-start | bytes 1572868
  150.6 4.6 %copy-start.19 = (bf16[256,1024]{1,0:T(8,128)(2,1)S(1)}, bf16[256,1024]{1,0:T(8,128)(2,1)}, u32[]{:S(2)}) copy-start(bf16[256,1024]{1,0:T(8,128)(2,1)} %copy-done.17) | copy-start | bytes 1572868
  151.9 4.1 %copy-start.26 = (bf16[256,1024]{1,0:T(8,128)(2,1)S(1)}, bf16[256,1024]{1,0:T(8,128)(2,1)}, u32[]{:S(2)}) copy-start(bf16[256,1024]{1,0:T(8,128)(2,1)} %copy-done.25) | copy-start | bytes 1572868
  151.9 4.6 %copy-start.28 = (bf16[256,1024]{1,0:T(8,128)(2,1)S(1)}, bf16[256,1024]{1,0:T(8,128)(2,1)}, u32[]{:S(2)}) copy-start(bf16[256,1024]{1,0:T(8,128)(2,1)} %copy-done.27) | copy-start | bytes 1572868
  151.9 4.8 %copy-start.30 = (bf16[256,1024]{1,0:T(8,128)(2,1)S(1)}, bf16[256,1024]{1,0:T(8,128)(2,1)}, u32[]{:S(2)}) copy-start(bf16[256,1024]{1,0:T(8,128)(2,1)} %copy-done.29) | copy-start | bytes 1572868
  151.9 5.0 %copy-start.32 = (bf16[256,1024]{1,0:T(8,128)(2,1)S(1)}, bf16[256,1024]{1,0:T(8,128)(2,1)}, u32[]{:S(2)}) copy-start(bf16[256,1024]{1,0:T(8,128)(2,1)} %copy-done.31) | copy-start | bytes 1572868
  153.3 3.9 %copy-start.34 = (bf16[256,1024]{1,0:T(8,128)(2,1)S(1)}, bf16[256,1024]{1,0:T(8,128)(2,1)}, u32[]{:S(2)}) copy-start(bf16[256,1024]{1,0:T(8,128)(2,1)} %copy-done.33) | copy-start | bytes 1572868
  153.5 3.8 %copy-start.36 = (bf16[256,1024]{1,0:T(8,128)(2,1)S(1)}, bf16[256,1024]{1,0:T(8,128)(2,1)}, u32[]{:S(2)}) copy-start(bf16[256,1024]{1,0:T(8,128)(2,1)} %copy-done.35) | copy-start | bytes 1572868
  155.2 2.4 %copy-start.38 = (bf16[256,1024]{1,0:T(8,128)(2,1)S(1)}, bf16[256,1024]{1,0:T(8,128)(2,1)}, u32[]{:S(2)}) copy-start(bf16[256,1024]{1,0:T(8,128)(2,1)} %copy-done.37) | copy-start | bytes 1572868
  155.4 2.4 %copy-start.40 = (bf16[256,1024]{1,0:T(8,128)(2,1)S(1)}, bf16[256,1024]{1,0:T(8,128)(2,1)}, u32[]{:S(2)}) copy-start(bf16[256,1024]{1,0:T(8,128)(2,1)} %copy-done.39) | copy-start | bytes 1572868
  156.7 2.9 %copy-start.74 = (u32[32]{0:T(128)S(1)}, u32[32]{0:T(128)}, u32[]{:S(2)}) copy-start(u32[32]{0:T(128)} %constant.60) | copy-start | bytes 388
  156.7 7.2 %copy-start.7 = (f32[96,1024]{1,0:T(8,128)S(1)}, f32[96,1024]{1,0:T(8,128)}, u32[]{:S(2)}) copy-start(f32[96,1024]{1,0:T(8,128)} %param.17) | copy-start | bytes 1179652
  (36 other events, 43.8 us)
Sparse Core Ops, SparseCore 0:
  135.7 8.4 reduce-scatter.3
  146.9 8.6 reduce-scatter.7
  158.4 8.8 reduce-scatter.5
where the time goes:
time: 175 us; the launch traced here: 174 us
  blocking collectives  66.8 us (38%)
  matrix products  48.8 us (28%)
  local copies, waits for them, and re-layouts  23.7 us (14%)
  between operations  16.4 us (9%)
  other arithmetic  15.8 us (9%)
  waiting for transfers between devices  1.95 us (1%)
    all_gather x1, blocking collectives, body(): lax.all_gather(local_proj[None], 'slab', axis=0, tiled=True)  32.2 us
    all_gather x1, blocking collectives, body(): lax.all_gather(slab_depth[None], 'slab', axis=0, tiled=True)  32.2 us
    unnamed x197, local copies, waits for them, and re-layouts  20.7 us
    dot_general x8, matrix products, hidden_layers(): jnp.dot(weight_b, first_act, preferred_element_type=jnp.float32)  12 us
    dot_general x8, matrix products, body(): jnp.einsum('hr,gr->hg', second_delta, first_act, preferred_element_type=j...  7.23 us
    dot_general x8, matrix products, body(): jnp.einsum('ch,cr->hr', weight_c, logit_block, preferred_element_type=jnp...  4.39 us
    dot_general x8, matrix products, hidden_layers(): jnp.dot(weight_a, inputs, preferred_element_type=jnp.float32)  4.36 us
    dot_general x8, matrix products, body(): jnp.einsum('hr,cr->hc', second_act, logit_block, preferred_element_type=j...  4.2 us
  transfers between devices with their start and end apart: 3, of which 1 were waited for; matrix products, arithmetic and copies ran while one was open for 12% of the time, Pallas kernels for 0%

commit v1 on v0

v1 whole, which is shorter than its diff:
```python
import functools

import jax
import jax.numpy as jnp
from jax import lax
from jax.experimental import pallas as pl
from jax.experimental.pallas import tpu as pltpu
from jax.sharding import PartitionSpec as P

MESH = pl.DeviceIdType.MESH
F32 = jnp.float32
BF16 = jnp.bfloat16


def dot(a, b):
    return jnp.dot(a, b, preferred_element_type=F32)


def dot_nt(a, b):
    return lax.dot_general(a, b, (((1,), (1,)), ((), ())), preferred_element_type=F32)


def main_kernel(
    slabs, chunks, unroll,
    x_ref, gap_ref, live_ref, dir_ref, cot_ref, w1_ref, b1_ref, w2_ref, b2_ref,
    wc_ref, bc_ref, wd_ref, bd_ref,
    feat_ref, dens_ref, sw_ref, g1_ref, g2_ref, gc_ref, gs_ref,
    xp, fp, perm, w1h, w1t, w2h, w2t, wch, wct,
    a1, s1, a2, s2, mix, raw_s, proj_s, ins_s, beh_s, rg_s, sww,
    gath, gsum, grecv, send_sem, recv_sem, wsem,
):
    slots = gap_ref.shape[0]
    rays = gap_ref.shape[1]
    feat = w1_ref.shape[1]
    hid = w1_ref.shape[0]
    ch = wc_ref.shape[0]
    rb = rays // chunks
    half = hid // 2
    me = lax.axis_index("slab")
    ray = lax.axis_index("ray")
    other = 1 - ray

    barrier = pltpu.get_barrier_semaphore()

    def greet(step, carry):
        pl.semaphore_signal(
            barrier, inc=1, device_id={"slab": lax.rem(me + step, slabs)}, device_id_type=MESH
        )
        return carry

    lax.fori_loop(1, slabs, greet, 0)
    pl.semaphore_signal(barrier, inc=1, device_id={"ray": other}, device_id_type=MESH)

    w1h[...] = w1_ref[...] * 0.5
    w2h[...] = w2_ref[...] * 0.5
    w1t[...] = w1_ref[...].astype(F32).T.astype(BF16)
    w2t[...] = (w2_ref[...].astype(F32) * 0.5).T.astype(BF16)
    pad = wch.shape[0] - ch
    wrow = jnp.where(
        lax.broadcasted_iota(jnp.int32, (pad, hid), 0) == 0, wd_ref[...].astype(F32) * 0.5, 0.0
    )
    wch[0:ch, :] = wc_ref[...] * 0.5
    wch[ch:, :] = wrow.astype(BF16)
    wct[...] = wch[...].astype(F32).T.astype(BF16)
    b1h = b1_ref[...] * 0.5
    b2h = b2_ref[...] * 0.5
    bch = bc_ref[...] * 0.5

    rows = slots * feat
    to = lax.broadcasted_iota(jnp.int32, (rows, rows), 0)
    at = lax.broadcasted_iota(jnp.int32, (rows, rows), 1)
    perm[...] = jnp.where(at == lax.rem(to, feat) * slots + to // feat, 1.0, 0.0).astype(BF16)

    gsum[...] = jnp.zeros_like(gsum)

    def forward(c):
        span = pl.ds(c * rb, rb)
        xp[c] = dot(perm[...], x_ref[:, span]).astype(BF16)
        cot = cot_ref[:, span]
        cot_q = cot * 0.25
        cot_sum = jnp.sum(cot, axis=0, keepdims=True)

        def step(k, carry):
            xk = xp[c, pl.ds(pl.multiple_of(k * feat, feat), feat), :]
            u = dot(w1h[...], xk) + b1h
            t = jnp.tanh(u)
            p = 1.0 + t
            a = u * p
            a1[c, k] = a.astype(BF16)
            s1[c, k] = (p + a * (1.0 - t)).astype(BF16)
            u = dot(w2h[...], a1[c, k]) + b2h
            t = jnp.tanh(u)
            p = 1.0 + t
            a = u * p
            a2[c, k] = a.astype(BF16)
            s2[c, k] = (p + a * (1.0 - t)).astype(BF16)
            l = dot(wch[...], a2[c, k])
            t = jnp.tanh(l[0:ch] + bch)
            mix[c, k] = cot_q - cot_q * t * t
            raw_s[c, pl.ds(k, 1), :] = l[ch : ch + 1] * 2.0 + bd_ref[...]
            proj_s[c, pl.ds(k, 1), :] = 0.5 * (
                cot_sum + jnp.sum(cot * t, axis=0, keepdims=True)
            )
            return carry

        lax.fori_loop(0, slots, step, 0, unroll=unroll)

    def depth_of(c):
        span = pl.ds(c * rb, rb)
        raw = raw_s[c]
        live = (
            lax.broadcasted_iota(jnp.int32, raw.shape, 0) < live_ref[:, span]
        ).astype(F32)
        scale = gap_ref[:, span] * live
        soft = jnp.maximum(raw, 0.0) + jnp.log1p(jnp.exp(-jnp.abs(raw)))
        return raw, scale, soft * scale

    def summarize(c):
        raw, scale, depth = depth_of(c)
        total = jnp.zeros((1, rb), F32)
        for k in range(slots):
            ins_s[c, k : k + 1, :] = total
            total = total + depth[k : k + 1]
        weight = jnp.exp(-ins_s[c]) * (1.0 - jnp.exp(-depth))
        gath[c, me, 0:1, :] = total
        gath[c, me, 1:2, :] = jnp.sum(weight * proj_s[c], axis=0, keepdims=True)

    def copy_to(c, step):
        return pltpu.make_async_remote_copy(
            src_ref=gath.at[c, me],
            dst_ref=gath.at[c, me],
            send_sem=send_sem.at[c, step],
            recv_sem=recv_sem.at[c, step],
            device_id={"slab": lax.rem(me + step, slabs)},
            device_id_type=MESH,
        )

    def send(c):
        def go(step, carry):
            copy_to(c, step).start()
            return carry

        lax.fori_loop(1, slabs, go, 0)

    def receive(c):
        def go(step, carry):
            copy_to(c, step).wait()
            return carry

        lax.fori_loop(1, slabs, go, 0)

    def settle(c):
        span = pl.ds(c * rb, rb)
        raw, scale, depth = depth_of(c)
        zero = jnp.zeros((1, rb), F32)
        before, after, up, down = zero, zero, zero, zero
        for s in range(slabs):
            tau = gath[c, s, 0:1, :]
            light = gath[c, s, 1:2, :]
            before = before + jnp.where(s < me, tau, 0.0)
            after = after + jnp.where(s > me, tau, 0.0)
            down = jnp.where(s < me, light + jnp.exp(-tau) * down, down)
        for s in reversed(range(slabs)):
            tau = gath[c, s, 0:1, :]
            light = gath[c, s, 1:2, :]
            up = jnp.where(s > me, light + jnp.exp(-tau) * up, up)
        ascend = dir_ref[:, span] == 0
        prefix = jnp.where(ascend, before, after)
        behind = jnp.where(ascend, up, down)
        behind_out = jnp.exp(-(prefix + gath[c, me, 0:1, :])) * behind
        transmit = jnp.exp(-(prefix + ins_s[c]))
        fade = jnp.exp(-depth)
        weight = transmit * (1.0 - fade)
        sww[c] = weight
        sw_ref[:, span] = weight
        proj = proj_s[c]
        carried = weight * proj
        total = behind_out
        for k in reversed(range(slots)):
            beh_s[c, k : k + 1, :] = total
            total = total + carried[k : k + 1]
        dens = (transmit * fade * proj - beh_s[c]) * scale
        dens_ref[:, span] = dens
        rg_s[c] = dens * (0.5 * jnp.tanh(0.5 * raw) + 0.5)

    def backward(c):
        first_row = lax.broadcasted_iota(jnp.int32, (pad, rb), 0) == 0

        def step(k, carry):
            lg = mix[c, k] * sww[c, pl.ds(k, 1), :]
            tail = jnp.where(first_row, rg_s[c, pl.ds(k, 1), :], 0.0)
            lga = jnp.concatenate([lg.astype(BF16), tail.astype(BF16)], axis=0)
            d2 = (dot(wct[...], lga) * s2[c, k].astype(F32)).astype(BF16)
            d1 = (dot(w2t[...], d2) * s1[c, k].astype(F32)).astype(BF16)
            at_k = pl.ds(pl.multiple_of(k * feat, feat), feat)
            fp[c, at_k, :] = dot(w1t[...], d1).astype(BF16)
            gsum[:, 0:hid] += dot_nt(d2, a1[c, k])
            gsum[:, hid : hid + ch + pad] += dot_nt(a2[c, k], lga)
            gsum[:, hid + ch + pad : hid + ch + pad + feat] += dot_nt(d1, xp[c, at_k, :])
            return carry

        lax.fori_loop(0, slots, step, 0, unroll=unroll)

    for c in range(chunks):
        forward(c)
        summarize(c)
        if c == 0:
            pl.semaphore_wait(barrier, slabs)
        send(c)
    for c in range(chunks):
        receive(c)
        settle(c)
        backward(c)

    give = pltpu.make_async_remote_copy(
        src_ref=gsum.at[pl.ds(pl.multiple_of(other * half, half), half)],
        dst_ref=grecv,
        send_sem=wsem.at[0],
        recv_sem=wsem.at[1],
        device_id={"ray": other},
        device_id_type=MESH,
    )
    give.start()
    for c in range(chunks):
        feat_ref[:, pl.ds(c * rb, rb)] = lax.dot_general(
            perm[...], fp[c], (((0,), (0,)), ((), ())), preferred_element_type=F32
        ).astype(BF16)
    give.wait()
    both = gsum[pl.ds(pl.multiple_of(ray * half, half), half), :] + grecv[...]
    g2_ref[...] = both[:, 0:hid]
    gc_ref[...] = both[:, hid : hid + ch]
    g1_ref[...] = both[:, hid + ch + pad : hid + ch + pad + feat]
    same = lax.broadcasted_iota(jnp.int32, (half, half), 0) == lax.broadcasted_iota(
        jnp.int32, (half, half), 1
    )
    gs_ref[...] = jnp.sum(
        jnp.where(same, both[:, hid + ch : hid + ch + 1], 0.0), axis=0, keepdims=True
    )


def body(
    slabs, features, spacing, live_counts, direction, cotangent, first_weight, first_bias,
    second_weight, second_bias, color_weight, color_bias, sigma_weight, sigma_bias,
):
    _, feat, slots, rays = features.shape
    hid = first_weight.shape[1]
    ch = color_weight.shape[1]
    padded = 128
    chunks = 2
    rb = rays // chunks
    half = hid // 2
    wide = hid + padded + 128
    rows = slots * feat
    vm = pl.BlockSpec(memory_space=pltpu.VMEM)
    S = jax.ShapeDtypeStruct
    V = pltpu.VMEM
    outs = pl.pallas_call(
        functools.partial(main_kernel, slabs, chunks, 2),
        out_shape=(
            S((rows, rays), BF16), S((slots, rays), F32), S((slots, rays), F32),
            S((half, feat), F32), S((half, hid), F32), S((half, ch), F32), S((1, half), F32),
        ),
        in_specs=[vm] * 13,
        out_specs=(vm,) * 7,
        scratch_shapes=[
            V((chunks, rows, rb), BF16), V((chunks, rows, rb), BF16), V((rows, rows), BF16),
            V((hid, feat), BF16), V((feat, hid), BF16), V((hid, hid), BF16), V((hid, hid), BF16),
            V((padded, hid), BF16), V((hid, padded), BF16),
            V((chunks, slots, hid, rb), BF16), V((chunks, slots, hid, rb), BF16),
            V((chunks, slots, hid, rb), BF16), V((chunks, slots, hid, rb), BF16),
            V((chunks, slots, ch, rb), F32),
            V((chunks, slots, rb), F32), V((chunks, slots, rb), F32), V((chunks, slots, rb), F32),
            V((chunks, slots, rb), F32), V((chunks, slots, rb), F32), V((chunks, slots, rb), F32),
            V((chunks, slabs, 2, rb), F32),
            V((hid, wide), F32), V((half, wide), F32),
            pltpu.SemaphoreType.DMA((chunks, slabs)),
            pltpu.SemaphoreType.DMA((chunks, slabs)),
            pltpu.SemaphoreType.DMA((2,)),
        ],
        compiler_params=pltpu.CompilerParams(
            collective_id=0, has_side_effects=True, vmem_limit_bytes=48 * 1024 * 1024
        ),
    )(
        features.reshape(rows, rays), spacing[0], live_counts, direction[None], cotangent,
        first_weight[0], first_bias.reshape(hid, 1), second_weight[0],
        second_bias.reshape(hid, 1), color_weight[0], color_bias.reshape(ch, 1),
        sigma_weight, sigma_bias.reshape(1, 1),
    )
    feature_grad, dens, weight, g1, g2, gc, gs = outs
    radiance_grad = (weight[None] * cotangent[:, None, :]).astype(BF16)
    return (
        feature_grad.reshape(1, feat, slots, rays), dens[None], radiance_grad[None],
        g1[None], g2[None], gc[None], gs,
    )


def solution(mesh):
    rays = P(("groups", "ray"))
    in_specs = (
        P("slab", None, None, ("groups", "ray")),
        P("slab", None, ("groups", "ray")),
        P("slab", ("groups", "ray")),
        rays,
        P(None, ("groups", "ray")),
        P("slab", None, None),
        P("slab", None),
        P("slab", None, None),
        P("slab", None),
        P("slab", None, None),
        P("slab", None),
        P("slab", None),
        P("slab"),
    )
    out_specs = (
        P("slab", None, None, ("groups", "ray")),
        P("slab", None, ("groups", "ray")),
        P("slab", None, None, ("groups", "ray")),
        P(("groups", "slab"), "ray", None),
        P(("groups", "slab"), "ray", None),
        P(("groups", "slab"), "ray", None),
        P(("groups", "slab"), "ray"),
    )
    return jax.shard_map(
        functools.partial(body, mesh.shape["slab"]),
        mesh=mesh,
        in_specs=in_specs,
        out_specs=out_specs,
        check_vma=False,
    )
```

time: 175 us -> 45 us (0.26)
  blocking collectives: 66.8 us -> 0 us
  matrix products: 48.8 us -> 0 us
  Pallas kernels: 0 us -> 27.5 us
  between operations: 16.4 us -> 1.38 us
  other arithmetic: 15.8 us -> 1.44 us
  local copies, waits for them, and re-layouts: 23.7 us -> 14.1 us
  waiting for transfers between devices: 1.95 us -> 0 us
    all_gather x2 -> x0, blocking collectives: 64.4 us -> none  [the longest x1 32.2 us: body(): lax.all_gather(local_proj[None], 'slab', axis=0, tiled=True)]
    dot_general x88 -> x0, matrix products: 48.8 us -> none  [the longest x8 12 us: hidden_layers(): jnp.dot(weight_b, first_act, preferred_element_type=jnp.float32)]
    pallas_call x0 -> x1, Pallas kernels: none -> 27.5 us  [body(): pl.pallas_call(functools.partial(main_kernel, slabs, chunks, 2), out_shap...]
    unnamed x197 -> x25, local copies, waits for them, and re-layouts: 20.7 us -> 11.8 us
    reduce_sum x5 -> x0, other arithmetic: 3.81 us -> none  [the longest x1 1.6 us: body(): local = jnp.sum((jnp.exp(-inside) * opacity)[None] * radiance, axis=1)]
    mul x11 -> x0, other arithmetic: 2.77 us -> none  [the longest x1 1.41 us: body(): (transmit * jnp.exp(-depth) * projected - behind_in - behind_out[None]) *...]
    unnamed x1 -> x0, blocking collectives: 2.47 us -> none
    reshape x0 -> x3, local copies, waits for them, and re-layouts: none -> 2.38 us  [the longest x1 0.81 us: body(): first_bias.reshape(hid, 1)]
  transfers between devices with their start and end apart: 3 -> 0, of which waited for: 1 -> 0; matrix products, arithmetic and copies ran while one was open for 12% -> 0% of each run, Pallas kernels for 0% -> 0%
where the time goes in v1:
time: 45 us; the launch traced here: 44.5 us
  Pallas kernels  27.5 us (61%)
  local copies, waits for them, and re-layouts  14.1 us (31%)
  other arithmetic  1.44 us (3%)
  between operations  1.38 us (3%)
    pallas_call x1, Pallas kernels, body(): pl.pallas_call(functools.partial(main_kernel, slabs, chunks, 2), out_shap...  27.5 us
    unnamed x25, local copies, waits for them, and re-layouts  11.8 us
    convert_element_type x1, other arithmetic, body(): radiance_grad = (weight[None] * cotangent[:, None, :]).astype(BF16)  1.44 us

profile of v1, /device:TPU:0, one launch (start us, length us, event | category | flops | bytes accessed | tf_op | source)
XLA Modules:
  0.0 44.5 jit_solution(2014756949241035077)
XLA Ops:
  0.6 0.0 copy-start.1
  1.3 0.8 %copy.27.bc_ref = f32[96,1]{1,0:T(8,128)S(1)} copy(f32[96,1]{0,1:T(1,128)} %bitcast.29) | data formatting | bytes 768 | tf_op jit(solution)/shard_map/reshape | solution.py:286
  2.1 0.9 %copy.24 = bf16[1,256,64]{2,1,0:T(8,128)(2,1)S(1)} copy(bf16[1,256,64]{1,2,0:T(8,128)(2,1)} %param.18) | data formatting | bytes 65536 | tf_op args[5]
  3.0 0.8 %copy.25.b1_ref = f32[256,1]{1,0:T(8,128)S(1)} copy(f32[256,1]{0,1:T(1,128)} %bitcast.27) | data formatting | bytes 2048 | tf_op jit(solution)/shard_map/reshape | solution.py:285
  3.8 0.8 %copy.26.b2_ref = f32[256,1]{1,0:T(8,128)S(1)} copy(f32[256,1]{0,1:T(1,128)} %bitcast.28) | data formatting | bytes 2048 | tf_op jit(solution)/shard_map/reshape | solution.py:286
  4.6 0.0 copy-start
  4.6 1.0 %copy-done = f32[96,1024]{1,0:T(8,128)S(1)} copy-done((f32[96,1024]{1,0:T(8,128)S(1)}, f32[96,1024]{1,0:T(8,128)}, u32[]{:S(2)}) %copy-start) | copy-done | bytes 393240
  5.6 0.0 copy-start.2
  5.6 1.2 %copy-done.2 = bf16[1,64,8,1024]{3,2,1,0:T(8,128)(2,1)S(1)} copy-done((bf16[1,64,8,1024]{3,2,1,0:T(8,128)(2,1)S(1)}, bf16[1,64,8,1024]{3,2,1,0:T(8,128)(2,1)}, u32[]{:S(2)}) %copy-start.2) | copy-done | bytes 1048600
  6.8 0.0 copy-start.3
  6.8 0.9 %copy-done.3 = bf16[1,256,256]{2,1,0:T(8,128)(2,1)S(1)} copy-done((bf16[1,256,256]{2,1,0:T(8,128)(2,1)S(1)}, bf16[1,256,256]{2,1,0:T(8,128)(2,1)}, u32[]{:S(2)}) %copy-start.3) | copy-done | bytes 131096
  7.7 0.0 copy-start.4
  7.7 0.8 %copy-done.4 = bf16[1,96,256]{2,1,0:T(8,128)(2,1)S(1)} copy-done((bf16[1,96,256]{2,1,0:T(8,128)(2,1)S(1)}, bf16[1,96,256]{2,1,0:T(8,128)(2,1)}, u32[]{:S(2)}) %copy-start.4) | copy-done | bytes 49176
  8.5 0.0 copy-start.5
  8.5 0.8 %copy-done.5 = f32[1,8,1024]{2,1,0:T(8,128)S(1)} copy-done((f32[1,8,1024]{2,1,0:T(8,128)S(1)}, f32[1,8,1024]{2,1,0:T(8,128)}, u32[]{:S(2)}) %copy-start.5) | copy-done | bytes 32792
  9.3 0.0 copy-start.6
  9.3 0.7 %copy-done.6 = s32[1,1024]{1,0:T(1,128)S(1)} copy-done((s32[1,1024]{1,0:T(1,128)S(1)}, s32[1,1024]{1,0:T(1,128)}, u32[]{:S(2)}) %copy-start.6) | copy-done | bytes 4120
  10.0 0.0 copy-start.7
  10.0 0.7 %copy-done.7 = s32[1024]{0:T(1024)S(1)} copy-done((s32[1024]{0:T(1024)S(1)}, s32[1024]{0:T(1024)}, u32[]{:S(2)}) %copy-start.7) | copy-done | bytes 4120
  10.7 0.0 copy-start.8
  10.7 0.7 %copy-done.8 = bf16[1,256]{1,0:T(2,128)(2,1)S(1)} copy-done((bf16[1,256]{1,0:T(2,128)(2,1)S(1)}, bf16[1,256]{1,0:T(2,128)(2,1)}, u32[]{:S(2)}) %copy-start.8) | copy-done | bytes 536
  11.3 27.5 %shard_map.180 = (bf16[512,1024]{1,0:T(8,128)(2,1)S(1)}, f32[8,1024]{1,0:T(8,128)S(1)}, f32[8,1024]{1,0:T(8,128)S(1)}, f32[128,64]{1,0:T(8,128)S(1)}, f32[128,25...) custom-call(bf16[512,1024]{1,0:T(8,128)(2,1)S(1)} %bitcast.16, f32[8,1024]{1,0:T(8,128)S(1)} %bitcast.24, ...), custom_call_target="tpu_custom_call" | custom-call | tf_op jit(solution)/shard_map/pallas_call | solution.py:257
  38.9 0.7 %copy.28 = f32[1,128,64]{1,2,0:T(8,128)} copy(f32[1,128,64]{2,1,0:T(8,128)S(1)} %bitcast.22) | data formatting | bytes 65536
  39.6 0.7 %copy.29 = f32[1,128,96]{1,2,0:T(8,128)} copy(f32[1,128,96]{2,1,0:T(8,128)S(1)} %bitcast.21) | data formatting | bytes 98304
  40.3 0.0 copy-done.1
  40.3 1.4 %multiply_convert_fusion = bf16[1,96,8,1024]{3,2,1,0:T(8,128)(2,1)} fusion(f32[96,1024]{1,0:T(8,128)S(1)} %copy-done.1, f32[8,1024]{1,0:T(8,128)S(1)} %get-tuple-element.16), kind=kLoop, calls=%fused_computation | loop fusion | flops 1572864 | bytes 1998848 | tf_op jit(solution)/shard_map/convert_element_type | solution.py:290
  41.7 1.0 %copy.35 = bf16[1,64,8,1024]{3,2,1,0:T(8,128)(2,1)} copy(bf16[1,64,8,1024]{3,2,1,0:T(8,128)(2,1)S(1)} %bitcast.17) | data formatting | bytes 2097152
  42.7 0.6 %copy.36 = f32[1,8,1024]{2,1,0:T(8,128)} copy(f32[1,8,1024]{2,1,0:T(8,128)S(1)} %bitcast.25) | data formatting | bytes 65536
  43.3 0.7 %copy.37 = f32[1,128,256]{2,1,0:T(8,128)} copy(f32[1,128,256]{2,1,0:T(8,128)S(1)} %bitcast.20) | data formatting | bytes 262144
  44.0 0.5 %copy.38 = f32[1,128]{1,0:T(1,128)} copy(f32[1,128]{1,0:T(1,128)S(1)} %get-tuple-element.48) | data formatting | bytes 1024
Async XLA Ops:
  0.6 39.6 %copy-start.1 = (f32[96,1024]{1,0:T(8,128)S(1)}, f32[96,1024]{1,0:T(8,128)}, u32[]{:S(2)}) copy-start(f32[96,1024]{1,0:T(8,128)} %cot_ref.1) | copy-start | bytes 1179652
  4.6 1.0 %copy-start = (f32[96,1024]{1,0:T(8,128)S(1)}, f32[96,1024]{1,0:T(8,128)}, u32[]{:S(2)}) copy-start(f32[96,1024]{1,0:T(8,128)} %cot_ref.1) | copy-start | bytes 1179652
  5.6 1.2 %copy-start.2 = (bf16[1,64,8,1024]{3,2,1,0:T(8,128)(2,1)S(1)}, bf16[1,64,8,1024]{3,2,1,0:T(8,128)(2,1)}, u32[]{:S(2)}) copy-start(bf16[1,64,8,1024]{3,2,1,0:T(8,128)(2,1)} %param.13) | copy-start | bytes 3145732
  6.8 0.9 %copy-start.3 = (bf16[1,256,256]{2,1,0:T(8,128)(2,1)S(1)}, bf16[1,256,256]{2,1,0:T(8,128)(2,1)}, u32[]{:S(2)}) copy-start(bf16[1,256,256]{2,1,0:T(8,128)(2,1)} %param.20) | copy-start | bytes 393220
  7.7 0.8 %copy-start.4 = (bf16[1,96,256]{2,1,0:T(8,128)(2,1)S(1)}, bf16[1,96,256]{2,1,0:T(8,128)(2,1)}, u32[]{:S(2)}) copy-start(bf16[1,96,256]{2,1,0:T(8,128)(2,1)} %param.22) | copy-start | bytes 147460
  8.5 0.8 %copy-start.5 = (f32[1,8,1024]{2,1,0:T(8,128)S(1)}, f32[1,8,1024]{2,1,0:T(8,128)}, u32[]{:S(2)}) copy-start(f32[1,8,1024]{2,1,0:T(8,128)} %param.14) | copy-start | bytes 98308
  9.3 0.7 %copy-start.6 = (s32[1,1024]{1,0:T(1,128)S(1)}, s32[1,1024]{1,0:T(1,128)}, u32[]{:S(2)}) copy-start(s32[1,1024]{1,0:T(1,128)} %live_ref.1) | copy-start | bytes 12292
  10.0 0.7 %copy-start.7 = (s32[1024]{0:T(1024)S(1)}, s32[1024]{0:T(1024)}, u32[]{:S(2)}) copy-start(s32[1024]{0:T(1024)} %param.16) | copy-start | bytes 12292
  10.7 0.7 %copy-start.8 = (bf16[1,256]{1,0:T(2,128)(2,1)S(1)}, bf16[1,256]{1,0:T(2,128)(2,1)}, u32[]{:S(2)}) copy-start(bf16[1,256]{1,0:T(2,128)(2,1)} %wd_ref.1) | copy-start | bytes 1540

commit v2 on v1

--- a/solution.py
+++ b/solution.py
@@ -10,6 +10,8 @@
 MESH = pl.DeviceIdType.MESH
 F32 = jnp.float32
 BF16 = jnp.bfloat16
+CHUNKS = 2
+UNROLL = 8
 
 
 def dot(a, b):
@@ -22,17 +24,19 @@
 
 def main_kernel(
     slabs, chunks, unroll,
+    bd_ref, x_hbm, gap_hbm, live_hbm, dir_hbm, cot_hbm, w1_hbm, b1_hbm, w2_hbm, b2_hbm,
+    wc_hbm, bc_hbm, wd_hbm,
+    feat_ref, dens_ref, sw_ref, g1_ref, g2_ref, gc_ref, gs_ref,
     x_ref, gap_ref, live_ref, dir_ref, cot_ref, w1_ref, b1_ref, w2_ref, b2_ref,
-    wc_ref, bc_ref, wd_ref, bd_ref,
-    feat_ref, dens_ref, sw_ref, g1_ref, g2_ref, gc_ref, gs_ref,
-    xp, fp, perm, w1h, w1t, w2h, w2t, wch, wct,
-    a1, s1, a2, s2, mix, raw_s, proj_s, ins_s, beh_s, rg_s, sww,
+    wc_ref, bc_ref, wd_ref, in_sem,
+    xp, fp, perm, permt, w1h, w1t, w2h, w2t, wch, wct,
+    a1, s1, a2, s2, d1_s, d2_s, mix, raw_s, proj_s, ins_s, beh_s, rg_s, sww,
     gath, gsum, grecv, send_sem, recv_sem, wsem,
 ):
     slots = gap_ref.shape[0]
     rays = gap_ref.shape[1]
-    feat = w1_ref.shape[1]
-    hid = w1_ref.shape[0]
+    feat = w1_ref.shape[0]
+    hid = w1_ref.shape[1]
     ch = wc_ref.shape[0]
     rb = rays // chunks
     half = hid // 2
@@ -40,6 +44,19 @@
     ray = lax.axis_index("ray")
     other = 1 - ray
 
+    loads = [
+        pltpu.make_async_copy(src, dst, in_sem.at[i])
+        for i, (src, dst) in enumerate(
+            (
+                (x_hbm, x_ref), (w1_hbm, w1_ref), (b1_hbm, b1_ref), (w2_hbm, w2_ref),
+                (b2_hbm, b2_ref), (wc_hbm, wc_ref), (bc_hbm, bc_ref), (wd_hbm, wd_ref),
+                (cot_hbm, cot_ref), (gap_hbm, gap_ref), (live_hbm, live_ref), (dir_hbm, dir_ref),
+            )
+        )
+    ]
+    for load in loads:
+        load.start()
+
     barrier = pltpu.get_barrier_semaphore()
 
     def greet(step, carry):
@@ -51,27 +68,30 @@
     lax.fori_loop(1, slabs, greet, 0)
     pl.semaphore_signal(barrier, inc=1, device_id={"ray": other}, device_id_type=MESH)
 
-    w1h[...] = w1_ref[...] * 0.5
+    first = lax.broadcasted_iota(jnp.int32, (feat, slots * feat), 0) * slots
+    at = lax.broadcasted_iota(jnp.int32, (feat, slots * feat), 1)
+    for k in range(slots):
+        perm[k * feat : (k + 1) * feat, :] = jnp.where(at == first + k, 1.0, 0.0).astype(BF16)
+    for load in loads[1:]:
+        load.wait()
+
+    w1h[...] = (w1_ref[...].astype(F32) * 0.5).T.astype(BF16)
     w2h[...] = w2_ref[...] * 0.5
-    w1t[...] = w1_ref[...].astype(F32).T.astype(BF16)
-    w2t[...] = (w2_ref[...].astype(F32) * 0.5).T.astype(BF16)
     pad = wch.shape[0] - ch
     wrow = jnp.where(
         lax.broadcasted_iota(jnp.int32, (pad, hid), 0) == 0, wd_ref[...].astype(F32) * 0.5, 0.0
     )
     wch[0:ch, :] = wc_ref[...] * 0.5
     wch[ch:, :] = wrow.astype(BF16)
-    wct[...] = wch[...].astype(F32).T.astype(BF16)
-    b1h = b1_ref[...] * 0.5
-    b2h = b2_ref[...] * 0.5
-    bch = bc_ref[...] * 0.5
-
-    rows = slots * feat
-    to = lax.broadcasted_iota(jnp.int32, (rows, rows), 0)
-    at = lax.broadcasted_iota(jnp.int32, (rows, rows), 1)
-    perm[...] = jnp.where(at == lax.rem(to, feat) * slots + to // feat, 1.0, 0.0).astype(BF16)
-
-    gsum[...] = jnp.zeros_like(gsum)
+
+    def column(row):
+        n = row.shape[1]
+        return jnp.broadcast_to(row * 0.5, (8, n)).T[:, 0:1]
+
+    b1h = column(b1_ref[...])
+    b2h = column(b2_ref[...])
+    bch = column(bc_ref[...])
+    loads[0].wait()
 
     def forward(c):
         span = pl.ds(c * rb, rb)
@@ -97,7 +117,7 @@
             l = dot(wch[...], a2[c, k])
             t = jnp.tanh(l[0:ch] + bch)
             mix[c, k] = cot_q - cot_q * t * t
-            raw_s[c, pl.ds(k, 1), :] = l[ch : ch + 1] * 2.0 + bd_ref[...]
+            raw_s[c, pl.ds(k, 1), :] = l[ch : ch + 1] * 2.0 + bd_ref[0]
             proj_s[c, pl.ds(k, 1), :] = 0.5 * (
                 cot_sum + jnp.sum(cot * t, axis=0, keepdims=True)
             )
@@ -186,20 +206,30 @@
     def backward(c):
         first_row = lax.broadcasted_iota(jnp.int32, (pad, rb), 0) == 0
 
-        def step(k, carry):
+        def color(k, carry):
             lg = mix[c, k] * sww[c, pl.ds(k, 1), :]
             tail = jnp.where(first_row, rg_s[c, pl.ds(k, 1), :], 0.0)
             lga = jnp.concatenate([lg.astype(BF16), tail.astype(BF16)], axis=0)
-            d2 = (dot(wct[...], lga) * s2[c, k].astype(F32)).astype(BF16)
-            d1 = (dot(w2t[...], d2) * s1[c, k].astype(F32)).astype(BF16)
+            d2_s[k] = (dot(wct[...], lga) * s2[c, k].astype(F32)).astype(BF16)
+            gsum[:, hid : hid + ch + pad] += dot_nt(a2[c, k], lga)
+            return carry
+
+        def second(k, carry):
+            d2 = d2_s[k]
+            d1_s[k] = (dot(w2t[...], d2) * s1[c, k].astype(F32)).astype(BF16)
+            gsum[:, 0:hid] += dot_nt(d2, a1[c, k])
+            return carry
+
+        def first(k, carry):
+            d1 = d1_s[k]
             at_k = pl.ds(pl.multiple_of(k * feat, feat), feat)
             fp[c, at_k, :] = dot(w1t[...], d1).astype(BF16)
-            gsum[:, 0:hid] += dot_nt(d2, a1[c, k])
-            gsum[:, hid : hid + ch + pad] += dot_nt(a2[c, k], lga)
             gsum[:, hid + ch + pad : hid + ch + pad + feat] += dot_nt(d1, xp[c, at_k, :])
             return carry
 
-        lax.fori_loop(0, slots, step, 0, unroll=unroll)
+        lax.fori_loop(0, slots, color, 0, unroll=unroll)
+        lax.fori_loop(0, slots, second, 0, unroll=unroll)
+        lax.fori_loop(0, slots, first, 0, unroll=unroll)
 
     for c in range(chunks):
         forward(c)
@@ -207,6 +237,13 @@
         if c == 0:
             pl.semaphore_wait(barrier, slabs)
         send(c)
+    to = lax.broadcasted_iota(jnp.int32, permt.shape, 0)
+    at = lax.broadcasted_iota(jnp.int32, permt.shape, 1)
+    permt[...] = jnp.where(to == lax.rem(at, feat) * slots + at // feat, 1.0, 0.0).astype(BF16)
+    gsum[...] = jnp.zeros_like(gsum)
+    w1t[...] = w1_ref[...]
+    w2t[...] = (w2_ref[...].astype(F32) * 0.5).T.astype(BF16)
+    wct[...] = wch[...].astype(F32).T.astype(BF16)
     for c in range(chunks):
         receive(c)
         settle(c)
@@ -222,20 +259,41 @@
     )
     give.start()
     for c in range(chunks):
-        feat_ref[:, pl.ds(c * rb, rb)] = lax.dot_general(
-            perm[...], fp[c], (((0,), (0,)), ((), ())), preferred_element_type=F32
-        ).astype(BF16)
+        feat_ref[:, pl.ds(c * rb, rb)] = dot(permt[...], fp[c]).astype(BF16)
     give.wait()
     both = gsum[pl.ds(pl.multiple_of(ray * half, half), half), :] + grecv[...]
     g2_ref[...] = both[:, 0:hid]
-    gc_ref[...] = both[:, hid : hid + ch]
-    g1_ref[...] = both[:, hid + ch + pad : hid + ch + pad + feat]
-    same = lax.broadcasted_iota(jnp.int32, (half, half), 0) == lax.broadcasted_iota(
-        jnp.int32, (half, half), 1
-    )
-    gs_ref[...] = jnp.sum(
-        jnp.where(same, both[:, hid + ch : hid + ch + 1], 0.0), axis=0, keepdims=True
-    )
+    turned = both[:, hid : hid + ch + pad].T
+    gc_ref[...] = turned[0:ch]
+    gs_ref[...] = turned[ch : ch + 1]
+    g1_ref[...] = both[:, hid + ch + pad :].T[0:feat]
+
+
+def write_kernel(
+    feat_ref, dens_ref, sw_ref, g1_ref, g2_ref, gc_ref, gs_ref, cot_ref,
+    feat_out, dens_out, rad_out, g1_out, g2_out, gc_out, gs_out,
+    rad, sem, rad_sem,
+):
+    ch = cot_ref.shape[0]
+    parts = rad_sem.shape[0]
+    each = ch // parts
+    pairs = (
+        (feat_ref, feat_out), (g2_ref, g2_out), (gc_ref, gc_out), (g1_ref, g1_out),
+        (dens_ref, dens_out), (gs_ref, gs_out),
+    )
+    copies = [pltpu.make_async_copy(src, dst, sem.at[i]) for i, (src, dst) in enumerate(pairs)]
+    for copy in copies:
+        copy.start()
+    weight = sw_ref[...]
+    for part in range(parts):
+        for c in range(part * each, (part + 1) * each):
+            rad[c] = (weight * cot_ref[c : c + 1, :]).astype(BF16)
+        span = pl.ds(part * each, each)
+        copy = pltpu.make_async_copy(rad.at[span], rad_out.at[span], rad_sem.at[part])
+        copy.start()
+        copies.append(copy)
+    for copy in copies:
+        copy.wait()
 
 
 def body(
@@ -246,28 +304,34 @@
     hid = first_weight.shape[1]
     ch = color_weight.shape[1]
     padded = 128
-    chunks = 2
+    chunks = CHUNKS
     rb = rays // chunks
     half = hid // 2
     wide = hid + padded + 128
     rows = slots * feat
     vm = pl.BlockSpec(memory_space=pltpu.VMEM)
+    hbm = pl.BlockSpec(memory_space=pltpu.HBM)
     S = jax.ShapeDtypeStruct
     V = pltpu.VMEM
     outs = pl.pallas_call(
-        functools.partial(main_kernel, slabs, chunks, 2),
+        functools.partial(main_kernel, slabs, chunks, UNROLL),
         out_shape=(
             S((rows, rays), BF16), S((slots, rays), F32), S((slots, rays), F32),
-            S((half, feat), F32), S((half, hid), F32), S((half, ch), F32), S((1, half), F32),
+            S((feat, half), F32), S((half, hid), F32), S((ch, half), F32), S((1, half), F32),
         ),
-        in_specs=[vm] * 13,
+        in_specs=[pl.BlockSpec(memory_space=pltpu.SMEM)] + [hbm] * 12,
         out_specs=(vm,) * 7,
         scratch_shapes=[
-            V((chunks, rows, rb), BF16), V((chunks, rows, rb), BF16), V((rows, rows), BF16),
+            V((rows, rays), BF16), V((slots, rays), F32), V((1, rays), jnp.int32),
+            V((1, rays), jnp.int32), V((ch, rays), F32), V((feat, hid), BF16), V((1, hid), F32),
+            V((hid, hid), BF16), V((1, hid), F32), V((ch, hid), BF16), V((1, ch), F32),
+            V((1, hid), BF16), pltpu.SemaphoreType.DMA((12,)),
+            V((chunks, rows, rb), BF16), V((chunks, rows, rb), BF16), V((rows, rows), BF16), V((rows, rows), BF16),
             V((hid, feat), BF16), V((feat, hid), BF16), V((hid, hid), BF16), V((hid, hid), BF16),
             V((padded, hid), BF16), V((hid, padded), BF16),
             V((chunks, slots, hid, rb), BF16), V((chunks, slots, hid, rb), BF16),
             V((chunks, slots, hid, rb), BF16), V((chunks, slots, hid, rb), BF16),
+            V((slots, hid, rb), BF16), V((slots, hid, rb), BF16),
             V((chunks, slots, ch, rb), F32),
             V((chunks, slots, rb), F32), V((chunks, slots, rb), F32), V((chunks, slots, rb), F32),
             V((chunks, slots, rb), F32), V((chunks, slots, rb), F32), V((chunks, slots, rb), F32),
@@ -281,16 +345,34 @@
             collective_id=0, has_side_effects=True, vmem_limit_bytes=48 * 1024 * 1024
         ),
     )(
-        features.reshape(rows, rays), spacing[0], live_counts, direction[None], cotangent,
-        first_weight[0], first_bias.reshape(hid, 1), second_weight[0],
-        second_bias.reshape(hid, 1), color_weight[0], color_bias.reshape(ch, 1),
-        sigma_weight, sigma_bias.reshape(1, 1),
-    )
-    feature_grad, dens, weight, g1, g2, gc, gs = outs
-    radiance_grad = (weight[None] * cotangent[:, None, :]).astype(BF16)
+        sigma_bias,
+        *(
+            pltpu.with_memory_space_constraint(value, pltpu.HBM)
+            for value in (
+                features.reshape(rows, rays), spacing[0], live_counts, direction[None],
+                cotangent, first_weight[0].T, first_bias, second_weight[0], second_bias,
+                color_weight[0], color_bias, sigma_weight,
+            )
+        ),
+    )
+    feature_grad, dens, radiance_grad, g1, g2, gc, gs = pl.pallas_call(
+        write_kernel,
+        out_shape=(
+            S((rows, rays), BF16), S((slots, rays), F32), S((ch, slots, rays), BF16),
+            S((feat, half), F32), S((half, hid), F32), S((ch, half), F32), S((1, half), F32),
+        ),
+        in_specs=[vm] * 8,
+        out_specs=(hbm,) * 7,
+        scratch_shapes=[
+            V((ch, slots, rays), BF16),
+            pltpu.SemaphoreType.DMA((6,)),
+            pltpu.SemaphoreType.DMA((4,)),
+        ],
+        compiler_params=pltpu.CompilerParams(vmem_limit_bytes=8 * 1024 * 1024),
+    )(*outs, cotangent)
     return (
         feature_grad.reshape(1, feat, slots, rays), dens[None], radiance_grad[None],
-        g1[None], g2[None], gc[None], gs,
+        g1.T[None], g2[None], gc.T[None], gs,
     )
 
 

time: 45 us -> 28.8 us (0.64)
  local copies, waits for them, and re-layouts: 14.1 us -> 0.01 us
  other arithmetic: 1.44 us -> 0 us
    unnamed x25 -> x2, local copies, waits for them, and re-layouts: 11.8 us -> 0.01 us
    reshape x3 -> x0, local copies, waits for them, and re-layouts: 2.38 us -> none  [the longest x1 0.81 us: body(): first_bias.reshape(hid, 1)]
    convert_element_type x1 -> x0, other arithmetic: 1.44 us -> none  [body(): radiance_grad = (weight[None] * cotangent[:, None, :]).astype(BF16)]
    pallas_call x1 -> x2, Pallas kernels: 27.5 us -> 27.1 us  [the longest x1 25.5 us: body(): pl.pallas_call(functools.partial(main_kernel, slabs, chunks, UNROLL), out...]
where the time goes in v2:
time: 28.8 us; the launch traced here: 28.6 us
  Pallas kernels  27.1 us (94%)
  between operations  1.52 us (5%)
    pallas_call x1, Pallas kernels, body(): pl.pallas_call(functools.partial(main_kernel, slabs, chunks, UNROLL), out...  25.5 us
    pallas_call x1, Pallas kernels, body(): pl.pallas_call(write_kernel, out_shape=(S((rows, rays), BF16), S((slots,...  1.66 us

profile of v2, /device:TPU:0, one launch (start us, length us, event | category | flops | bytes accessed | tf_op | source)
XLA Modules:
  0.0 28.6 jit_solution(501203049259165657)
XLA Ops:
  0.6 0.0 copy-start
  1.3 25.5 %shard_map.180 = (bf16[512,1024]{1,0:T(8,128)(2,1)S(1)}, f32[8,1024]{1,0:T(8,128)S(1)}, f32[8,1024]{1,0:T(8,128)S(1)}, f32[64,128]{1,0:T(8,128)S(1)}, f32[128,25...) custom-call(f32[1]{0:T(128)S(6)} %copy.20.bd_ref, bf16[512,1024]{1,0:T(8,128)(2,1)} %bitcast.18, ...), custom_call_target="tpu_custom_call" | custom-call | tf_op jit(solution)/shard_map/pallas_call | solution.py:316
  26.8 0.0 copy-done
  26.8 1.7 %shard_map.181 = (bf16[512,1024]{1,0:T(8,128)(2,1)}, f32[8,1024]{1,0:T(8,128)}, bf16[96,8,1024]{2,1,0:T(8,128)(2,1)}, f32[64,128]{1,0:T(8,128)}, f32[128,256]{1,...) custom-call(bf16[512,1024]{1,0:T(8,128)(2,1)S(1)} %get-tuple-element.21.feat_ref, ...), custom_call_target="tpu_custom_call" | custom-call | tf_op jit(solution)/shard_map/pallas_call | solution.py:358
Async XLA Ops:
  0.6 26.2 %copy-start = (f32[96,1024]{1,0:T(8,128)S(1)}, f32[96,1024]{1,0:T(8,128)}, u32[]{:S(2)}) copy-start(f32[96,1024]{1,0:T(8,128)} %cot_ref.1) | copy-start | bytes 1179652

commit v3 on v2

--- a/solution.py
+++ b/solution.py
@@ -44,6 +44,17 @@
     ray = lax.axis_index("ray")
     other = 1 - ray
 
+    barrier = pltpu.get_barrier_semaphore()
+
+    def greet(step, carry):
+        pl.semaphore_signal(
+            barrier, inc=1, device_id={"slab": lax.rem(me + step, slabs)}, device_id_type=MESH
+        )
+        return carry
+
+    lax.fori_loop(1, slabs, greet, 0, unroll=min(slabs - 1, 7))
+    pl.semaphore_signal(barrier, inc=1, device_id={"ray": other}, device_id_type=MESH)
+
     loads = [
         pltpu.make_async_copy(src, dst, in_sem.at[i])
         for i, (src, dst) in enumerate(
@@ -57,17 +68,6 @@
     for load in loads:
         load.start()
 
-    barrier = pltpu.get_barrier_semaphore()
-
-    def greet(step, carry):
-        pl.semaphore_signal(
-            barrier, inc=1, device_id={"slab": lax.rem(me + step, slabs)}, device_id_type=MESH
-        )
-        return carry
-
-    lax.fori_loop(1, slabs, greet, 0)
-    pl.semaphore_signal(barrier, inc=1, device_id={"ray": other}, device_id_type=MESH)
-
     first = lax.broadcasted_iota(jnp.int32, (feat, slots * feat), 0) * slots
     at = lax.broadcasted_iota(jnp.int32, (feat, slots * feat), 1)
     for k in range(slots):
@@ -100,7 +100,7 @@
         cot_q = cot * 0.25
         cot_sum = jnp.sum(cot, axis=0, keepdims=True)
 
-        def step(k, carry):
+        def first(k, carry):
             xk = xp[c, pl.ds(pl.multiple_of(k * feat, feat), feat), :]
             u = dot(w1h[...], xk) + b1h
             t = jnp.tanh(u)
@@ -108,12 +108,18 @@
             a = u * p
             a1[c, k] = a.astype(BF16)
             s1[c, k] = (p + a * (1.0 - t)).astype(BF16)
+            return carry
+
+        def second(k, carry):
             u = dot(w2h[...], a1[c, k]) + b2h
             t = jnp.tanh(u)
             p = 1.0 + t
             a = u * p
             a2[c, k] = a.astype(BF16)
             s2[c, k] = (p + a * (1.0 - t)).astype(BF16)
+            return carry
+
+        def color(k, carry):
             l = dot(wch[...], a2[c, k])
             t = jnp.tanh(l[0:ch] + bch)
             mix[c, k] = cot_q - cot_q * t * t
@@ -123,7 +129,9 @@
             )
             return carry
 
-        lax.fori_loop(0, slots, step, 0, unroll=unroll)
+        lax.fori_loop(0, slots, first, 0, unroll=unroll)
+        lax.fori_loop(0, slots, second, 0, unroll=unroll)
+        lax.fori_loop(0, slots, color, 0, unroll=unroll)
 
     def depth_of(c):
         span = pl.ds(c * rb, rb)
@@ -160,14 +168,14 @@
             copy_to(c, step).start()
             return carry
 
-        lax.fori_loop(1, slabs, go, 0)
+        lax.fori_loop(1, slabs, go, 0, unroll=min(slabs - 1, 7))
 
     def receive(c):
         def go(step, carry):
             copy_to(c, step).wait()
             return carry
 
-        lax.fori_loop(1, slabs, go, 0)
+        lax.fori_loop(1, slabs, go, 0, unroll=min(slabs - 1, 7))
 
     def settle(c):
         span = pl.ds(c * rb, rb)

time: 28.8 us -> 24.5 us (0.85)
  Pallas kernels: 27.1 us -> 22.9 us
    pallas_call x1, Pallas kernels: 25.5 us -> 21.2 us  [body(): pl.pallas_call(functools.partial(main_kernel, slabs, chunks, UNROLL), out...]
where the time goes in v3:
time: 24.5 us; the launch traced here: 24.4 us
  Pallas kernels  22.9 us (93%)
  between operations  1.52 us (6%)
    pallas_call x1, Pallas kernels, body(): pl.pallas_call(functools.partial(main_kernel, slabs, chunks, UNROLL), out...  21.2 us
    pallas_call x1, Pallas kernels, body(): pl.pallas_call(write_kernel, out_shape=(S((rows, rays), BF16), S((slots,...  1.66 us

profile of v3, /device:TPU:0, one launch (start us, length us, event | category | flops | bytes accessed | tf_op | source)
XLA Modules:
  0.0 24.4 jit_solution(3369792431365243807)
XLA Ops:
  0.6 0.0 copy-start
  1.3 21.2 %shard_map.180 = (bf16[512,1024]{1,0:T(8,128)(2,1)S(1)}, f32[8,1024]{1,0:T(8,128)S(1)}, f32[8,1024]{1,0:T(8,128)S(1)}, f32[64,128]{1,0:T(8,128)S(1)}, f32[128,25...) custom-call(f32[1]{0:T(128)S(6)} %copy.20.bd_ref, bf16[512,1024]{1,0:T(8,128)(2,1)} %bitcast.18, ...), custom_call_target="tpu_custom_call" | custom-call | tf_op jit(solution)/shard_map/pallas_call | solution.py:324
  22.5 0.0 copy-done
  22.6 1.7 %shard_map.181 = (bf16[512,1024]{1,0:T(8,128)(2,1)}, f32[8,1024]{1,0:T(8,128)}, bf16[96,8,1024]{2,1,0:T(8,128)(2,1)}, f32[64,128]{1,0:T(8,128)}, f32[128,256]{1,...) custom-call(bf16[512,1024]{1,0:T(8,128)(2,1)S(1)} %get-tuple-element.21.feat_ref, ...), custom_call_target="tpu_custom_call" | custom-call | tf_op jit(solution)/shard_map/pallas_call | solution.py:366
Async XLA Ops:
  0.6 21.9 %copy-start = (f32[96,1024]{1,0:T(8,128)S(1)}, f32[96,1024]{1,0:T(8,128)}, u32[]{:S(2)}) copy-start(f32[96,1024]{1,0:T(8,128)} %cot_ref.1) | copy-start | bytes 1179652
